TPU v7x, 256 devices: a whole 4x4x8 slice. The times are simulated.
256 devices in a mesh: frame: 32 (over y, z), head: 8 (over x, core).
Axes of the slice: x: 4, y: 4, z: 8, core: 2. Of those that a mesh axis runs over, the one named last changes fastest.
Arguments:
- queries: bfloat16 [32768, 5120], P('frame', 'head'), may hold values from -120 to 120
- key_states: bfloat16 [32768, 5120], P('frame', 'head'), may hold values from -6 to 6
- value_states: bfloat16 [32768, 5120], P('frame', 'head'), may hold values from -6 to 6
- out_weight: bfloat16 [5120, 5120], P('frame', 'head'), may hold values from -0.078125 to 0.078125
- head_labels: int32 [40], replicated, may hold values from 0 to 1, as said below
Outputs:
- projected: bfloat16 [32768, 5120], P('frame', 'head')
Inputs may be any that keep to these rules, and one draw needn't show every extreme that they name: `head_labels`: every 5 heads in a row (heads g * 5 to g * 5 + 4) hold 3 or 2 temporal heads; some such group holds 3, some other 2.
All inputs are finite; a program needn't handle non-finite values.
Results may differ from a plain program's by a relative error of at most 0.015.
Values may be sent and summed in bfloat16 or wider, within the bound.
A program may use at most 128 MiB of HBM per device.

v0:
```python
import jax
import jax.numpy as jnp
from jax import lax
from jax.sharding import PartitionSpec as P

HDIM = 128


def attend_heads(query_rows, key_rows, value_rows):
    scale = query_rows.shape[-1] ** (-0.5)
    scores = (
        jnp.einsum("...ld,...md->...lm", query_rows, key_rows, preferred_element_type=jnp.float32)
        * scale
    )
    largest = jnp.max(scores, axis=-1, keepdims=True)
    expo = jnp.exp(scores - largest)
    weights = (expo / jnp.sum(expo, axis=-1, keepdims=True)).astype(jnp.bfloat16)
    mixed_output = jnp.einsum(
        "...lm,...md->...ld", weights, value_rows, preferred_element_type=jnp.float32
    )
    return mixed_output.astype(jnp.bfloat16)


def placement(picked, keep, head_count):
    match = picked[:, None] == jnp.arange(head_count, dtype=jnp.int32)[None, :]
    return (match & keep[:, None]).astype(jnp.bfloat16)


def temporal_block(pieces):
    query_rows, key_rows, value_rows = pieces
    mixed_output = attend_heads(
        query_rows.transpose(1, 2, 0, 3),
        key_rows.transpose(1, 2, 0, 3),
        value_rows.transpose(1, 2, 0, 3),
    )
    mixed_output = mixed_output.transpose(2, 0, 1, 3)
    return lax.all_to_all(mixed_output, "frame", split_axis=0, concat_axis=1, tiled=True)


def per_device(queries, key_states, value_states, out_weight, head_labels):
    tok_rows = queries.shape[0]
    head_count = queries.shape[1] // HDIM
    top_temporal = head_count // 2 + 1
    top_spatial = head_count - top_temporal + 1
    first_head = lax.axis_index("head") * head_count
    local_labels = lax.dynamic_slice_in_dim(head_labels, first_head, head_count)
    query_heads = queries.reshape(tok_rows, head_count, HDIM)
    key_heads = key_states.reshape(tok_rows, head_count, HDIM)
    value_per_head = value_states.reshape(tok_rows, head_count, HDIM)
    order_spatial = jnp.argsort(local_labels, stable=True)[:top_spatial]
    keep_spatial = local_labels[order_spatial] == 0
    spatial_out = attend_heads(
        jnp.take(query_heads, order_spatial, axis=1).transpose(1, 0, 2),
        jnp.take(key_heads, order_spatial, axis=1).transpose(1, 0, 2),
        jnp.take(value_per_head, order_spatial, axis=1).transpose(1, 0, 2),
    )
    combined = jnp.einsum(
        "spd,sh->phd",
        spatial_out,
        placement(order_spatial, keep_spatial, head_count),
        preferred_element_type=jnp.float32,
    )
    picked = jnp.arange(head_count, dtype=jnp.int32)
    keep_temporal = local_labels[picked] == 1
    sent = (
        jnp.take(query_heads, picked, axis=1)[None],
        jnp.take(key_heads, picked, axis=1)[None],
        jnp.take(value_per_head, picked, axis=1)[None],
    )
    temporal_out = temporal_block(
        (
            lax.all_to_all(sent[0], "frame", split_axis=1, concat_axis=0, tiled=True),
            lax.all_to_all(sent[1], "frame", split_axis=1, concat_axis=0, tiled=True),
            lax.all_to_all(sent[2], "frame", split_axis=1, concat_axis=0, tiled=True),
        )
    )[0]
    combined = combined + jnp.einsum(
        "psd,sh->phd",
        temporal_out,
        placement(picked, keep_temporal, head_count),
        preferred_element_type=jnp.float32,
    )
    attended = combined.astype(jnp.bfloat16).reshape(tok_rows, head_count * HDIM)
    all_heads = lax.all_gather(attended, "head", axis=1, tiled=True)
    result = jnp.dot(
        all_heads,
        lax.all_gather(out_weight, "frame", axis=0, tiled=True),
        preferred_element_type=jnp.float32,
    )
    return result.astype(jnp.bfloat16)


def solution(mesh):
    return jax.shard_map(
        per_device,
        mesh=mesh,
        in_specs=(
            P("frame", "head"),
            P("frame", "head"),
            P("frame", "head"),
            P("frame", "head"),
            P(),
        ),
        out_specs=P("frame", "head"),
        check_vma=False,
    )
```

profile of v0, /device:TPU:1, one launch (start us, length us, event | category | flops | bytes accessed | tf_op | source)
XLA Modules:
  0.0 357.3 jit_solution(15219050363331854428)
XLA Ops:
  6.5 0.0 all-gather.5.cloned.1.call-start
  6.5 0.7 all-gather.5.cloned.1.call-update
  7.3 1.6 copy.50
  8.9 0.8 copy.51
  9.7 2.4 copy.48
  12.1 1.8 copy.49
  13.9 2.4 copy.52
  16.3 2.5 copy.53
  18.8 1.9 gather_fusion.5
  20.7 1.8 gather_fusion.6
  22.5 3.2 gather_fusion.7
  25.7 4.1 %select_bitcast_fusion = (bf16[1,1024,5,128]{3,1,2,0:T(8,128)(2,1)}, bf16[1,1024,5,128]{3,1,2,0:T(8,128)(2,1)}, bf16[1,1024,5,128]{3,1,2,0:T(8,128)(2,1)S(1)}) fusion(bf16[5,1024,128]{2,1,0:T(8,128)(2,1)} %gather_fusion.7, pred[5]{0:T(512)(128)(4,1)S(1)} %iota_compare_fusion.2, bf16[5,1024,128]{2,1,0:T(8,128)(2,1)} %gather_fusion.6, ...), kind=kLoop, calls=%fused_computation.35 | loop fusion | flops 1966080 | bytes 7864325 | tf_op jit(solution)/shard_map/broadcast_in_dim | solution.py:68
  29.8 2.2 copy.57
  32.1 12.1 %all-to-all-start = ((bf16[1,1024,5,128]{3,2,0,1:T(8,128)(2,1)}), bf16[1,1024,5,128]{3,2,0,1:T(8,128)(2,1)}, u32[]{:S(2)}, u32[]{:S(2)}) async-start(bf16[1,1024,5,128]{3,2,0,1:T(8,128)(2,1)} %copy.57), calls=%async_computation | async-start | bytes 4194304 | tf_op jit(solution)/shard_map/all_to_all | solution.py:72
  44.1 3.6 %copy.61 = bf16[1,1024,5,128]{3,2,0,1:T(8,128)(2,1)} copy(bf16[1,1024,5,128]{3,1,2,0:T(8,128)(2,1)} %get-tuple-element.12) | data formatting | bytes 2621440 | tf_op jit(solution)/shard_map/broadcast_in_dim | solution.py:67
  47.7 54.3 %all-to-all-done = bf16[1,1024,5,128]{3,2,0,1:T(8,128)(2,1)} async-done(((bf16[1,1024,5,128]{3,2,0,1:T(8,128)(2,1)}), bf16[1,1024,5,128]{3,2,0,1:T(8,128)(2,1)}, u32[]{:S(2)}, u32[]{:S(2)}) %all-to-all-start) | async-done | bytes 1310752 | tf_op jit(solution)/shard_map/all_to_all | solution.py:72
  102.1 11.6 %all-to-all-start.1 = ((bf16[1,1024,5,128]{3,2,0,1:T(8,128)(2,1)}), bf16[1,1024,5,128]{3,2,0,1:T(8,128)(2,1)}, u32[]{:S(2)}, u32[]{:S(2)}) async-start(bf16[1,1024,5,128]{3,2,0,1:T(8,128)(2,1)} %copy.61), calls=%async_computation.1 | async-start | bytes 4194304 | tf_op jit(solution)/shard_map/all_to_all | solution.py:73
  113.7 3.6 %copy.65 = bf16[1,1024,5,128]{3,2,0,1:T(8,128)(2,1)} copy(bf16[1,1024,5,128]{3,1,2,0:T(8,128)(2,1)} %get-tuple-element.11) | data formatting | bytes 2621440 | tf_op jit(solution)/shard_map/broadcast_in_dim | solution.py:68
  117.3 55.0 %all-to-all-done.1 = bf16[1,1024,5,128]{3,2,0,1:T(8,128)(2,1)} async-done(((bf16[1,1024,5,128]{3,2,0,1:T(8,128)(2,1)}), bf16[1,1024,5,128]{3,2,0,1:T(8,128)(2,1)}, u32[]{:S(2)}, u32[]{:S(2)}) %all-to-all-start.1) | async-done | bytes 1310752 | tf_op jit(solution)/shard_map/all_to_all | solution.py:73
  172.3 5.4 %all-to-all-start.2 = ((bf16[1,1024,5,128]{3,2,0,1:T(8,128)(2,1)}), bf16[1,1024,5,128]{3,2,0,1:T(8,128)(2,1)}, u32[]{:S(2)}, u32[]{:S(2)}) async-start(bf16[1,1024,5,128]{3,2,0,1:T(8,128)(2,1)} %copy.65), calls=%async_computation.2 | async-start | bytes 4194304 | tf_op jit(solution)/shard_map/all_to_all | solution.py:74
  177.7 0.0 copy-done.2
  177.8 0.1 dynamic_slice.3
  177.8 1.0 sort.17
  178.8 1.6 gather_fusion.3
  180.4 1.6 gather_fusion.2
  181.9 0.7 gather_fusion.4
  182.7 0.6 gather_fusion
  183.3 0.6 gather_fusion.1
  184.0 4.3 %fusion.20 = f32[32,5,32,32]{2,3,1,0:T(8,128)S(1)} fusion(bf16[32,32,5,128]{3,2,1,0:T(8,128)(2,1)} %bitcast.17, bf16[32,32,5,128]{3,2,1,0:T(8,128)(2,1)} %bitcast.13), kind=kOutput, calls=%fused_computation.30 | convolution fusion | flops 41943040 | bytes 3276800 | tf_op jit(solution)/shard_map/...ld,...md->...lm/dot_general | solution.py:12
  188.2 6.0 %fusion.50 = (f32[32,5,32]{2,1,0:T(8,128)S(1)}, f32[32,5,32,32]{2,3,1,0:T(8,128)S(1)}) fusion(f32[32,5,32,32]{2,3,1,0:T(8,128)S(1)} %fusion.20), kind=kOutput, calls=%fused_computation.70 | output fusion | flops 655391 | bytes 1331200 | tf_op jit(solution)/shard_map/sub | solution.py:16
  194.2 32.0 %all-to-all-done.2 = bf16[1,1024,5,128]{3,2,0,1:T(8,128)(2,1)} async-done(((bf16[1,1024,5,128]{3,2,0,1:T(8,128)(2,1)}), bf16[1,1024,5,128]{3,2,0,1:T(8,128)(2,1)}, u32[]{:S(2)}, u32[]{:S(2)}) %all-to-all-start.2) | async-done | bytes 1310752 | tf_op jit(solution)/shard_map/all_to_all | solution.py:74
  226.2 2.9 fusion.16
  229.1 0.0 copy-start.1
  229.1 1.6 copy.69
  230.7 7.1 %all-to-all-start.3 = ((bf16[32,32,5,128]{3,1,2,0:T(8,128)(2,1)}), bf16[32,32,5,128]{3,1,2,0:T(8,128)(2,1)S(1)}, u32[]{:S(2)}, u32[]{:S(2)}) async-start(bf16[32,32,5,128]{3,1,2,0:T(8,128)(2,1)} %copy.69), calls=%async_computation.3 | async-start | bytes 2621440 | tf_op jit(solution)/shard_map/all_to_all | solution.py:37
  237.8 0.0 all-gather.3.cloned.1.call-start
  237.8 0.0 copy-done.1
  237.8 9.8 %fusion.49 = (f32[3,1024]{1,0:T(4,128)S(1)}, f32[3,1024,1024]{1,2,0:T(8,128)}) fusion(bf16[3,1024,128]{2,1,0:T(8,128)(2,1)} %gather_fusion.2, pred[3]{0:T(512)(128)(4,1)S(1)} %get-tuple-element.9, bf16[3,1024,128]{2,1,0:T(8,128)(2,1)S(1)} %copy-done.1), kind=kOutput, calls=%fused_computation.69 | convolution fusion | flops 815531008 | bytes 14168067 | tf_op jit(solution)/shard_map/sub | solution.py:16
  247.6 6.9 %fusion.17 = bf16[3,1024,128]{2,1,0:T(8,128)(2,1)S(1)} fusion(f32[3,1024,1024]{1,2,0:T(8,128)} %get-tuple-element.15, f32[3,1024]{1,0:T(4,128)S(1)} %get-tuple-element.14, bf16[3,1024,128]{2,1,0:T(8,128)(2,1)S(1)} %gather_fusion.4, pred[3]{0:T(512)(128)(4,1)S(1)} %get-tuple-element.9), kind=kOutput, calls=%fused_computation.27 | convolution fusion | flops 812384256 | bytes 14168067 | tf_op jit(solution)/shard_map/...lm,...md->...ld/dot_general | solution.py:18
  254.5 6.8 %fusion.27 = f32[5,1024,128]{2,0,1:T(8,128)} fusion(bf16[3,1024,128]{2,1,0:T(8,128)(2,1)S(1)} %fusion.17, s32[3]{0:T(128)S(1)} %bitcast.56, pred[3]{0:T(512)(128)(4,1)S(1)} %broadcast_compare_fusion.1), kind=kOutput, calls=%fused_computation.40 | convolution fusion | flops 3932190 | bytes 3407887 | tf_op jit(solution)/shard_map/spd,sh->phd/dot_general | solution.py:57
  261.3 7.7 %all-to-all-done.3 = bf16[32,32,5,128]{3,1,2,0:T(8,128)(2,1)S(1)} async-done(((bf16[32,32,5,128]{3,1,2,0:T(8,128)(2,1)}), bf16[32,32,5,128]{3,1,2,0:T(8,128)(2,1)S(1)}, u32[]{:S(2)}, u32[]{:S(2)}) %all-to-all-start.3) | async-done | bytes 1310752 | tf_op jit(solution)/shard_map/all_to_all | solution.py:37
  269.0 0.3 copy.70
  269.3 3.4 fusion.13
  272.6 2.5 copy.72
  275.2 0.0 all-gather.3.cloned.1.call-update
  275.2 0.0 all-gather.5.cloned.1.call-done
  275.2 61.4 %all-gather.3.cloned.1.call-done = bf16[1024,5120]{0,1:T(8,128)(2,1)} async-done(((bf16[1024,640]{0,1:T(8,128)(2,1)}), bf16[1024,5120]{0,1:T(8,128)(2,1)}) %all-gather.3.cloned.1.call-update) | async-done | bytes 10485776 | tf_op jit(solution)/shard_map/all_gather | solution.py:84
  336.6 13.8 %convolution_convert_fusion = bf16[1024,640]{1,0:T(8,128)(2,1)} fusion(bf16[1024,5120]{0,1:T(8,128)(2,1)} %all-gather.3.cloned.1.call-done, bf16[5120,640]{1,0:T(8,128)(2,1)} %all-gather.5.cloned.1.call-done), kind=kOutput, calls=%fused_computation.24 | convolution fusion | flops 6711541760 | bytes 18350080 | tf_op jit(solution)/shard_map/dot_general | solution.py:85
  (11 shorter events, 0.0 us)
Async XLA Ops:
  6.5 268.7 %all-gather.5.cloned.1.call-start = ((), (), s32[]{:S(2)}) async-start(), calls=%async_computation.5 | async-start | bytes 6758400 | tf_op jit(solution)/shard_map/all_gather | solution.py:87
  32.1 70.0 %all-to-all-start = ((bf16[1,1024,5,128]{3,2,0,1:T(8,128)(2,1)}), bf16[1,1024,5,128]{3,2,0,1:T(8,128)(2,1)}, u32[]{:S(2)}, u32[]{:S(2)}) async-start(bf16[1,1024,5,128]{3,2,0,1:T(8,128)(2,1)} %copy.57), calls=%async_computation | async-start | bytes 4194304 | tf_op jit(solution)/shard_map/all_to_all | solution.py:72
  102.1 70.3 %all-to-all-start.1 = ((bf16[1,1024,5,128]{3,2,0,1:T(8,128)(2,1)}), bf16[1,1024,5,128]{3,2,0,1:T(8,128)(2,1)}, u32[]{:S(2)}, u32[]{:S(2)}) async-start(bf16[1,1024,5,128]{3,2,0,1:T(8,128)(2,1)} %copy.61), calls=%async_computation.1 | async-start | bytes 4194304 | tf_op jit(solution)/shard_map/all_to_all | solution.py:73
  117.3 60.5 %copy-start.2 = (s32[40]{0:T(128)S(1)}, s32[40]{0:T(128)}, u32[]{:S(2)}) copy-start(s32[40]{0:T(128)} %param.13) | copy-start | bytes 484
  172.3 53.9 %all-to-all-start.2 = ((bf16[1,1024,5,128]{3,2,0,1:T(8,128)(2,1)}), bf16[1,1024,5,128]{3,2,0,1:T(8,128)(2,1)}, u32[]{:S(2)}, u32[]{:S(2)}) async-start(bf16[1,1024,5,128]{3,2,0,1:T(8,128)(2,1)} %copy.65), calls=%async_computation.2 | async-start | bytes 4194304 | tf_op jit(solution)/shard_map/all_to_all | solution.py:74
  180.4 1.6 copy-start
  229.1 8.8 %copy-start.1 = (bf16[3,1024,128]{2,1,0:T(8,128)(2,1)S(1)}, bf16[3,1024,128]{2,1,0:T(8,128)(2,1)}, u32[]{:S(2)}) copy-start(bf16[3,1024,128]{2,1,0:T(8,128)(2,1)} %gather_fusion.3) | copy-start | bytes 2359300
  230.7 38.4 %all-to-all-start.3 = ((bf16[32,32,5,128]{3,1,2,0:T(8,128)(2,1)}), bf16[32,32,5,128]{3,1,2,0:T(8,128)(2,1)S(1)}, u32[]{:S(2)}, u32[]{:S(2)}) async-start(bf16[32,32,5,128]{3,1,2,0:T(8,128)(2,1)} %copy.69), calls=%async_computation.3 | async-start | bytes 2621440 | tf_op jit(solution)/shard_map/all_to_all | solution.py:37
  237.8 98.9 %all-gather.3.cloned.1.call-start = ((), (), s32[]{:S(2)}) async-start(), calls=%async_computation.4 | async-start | bytes 11796480 | tf_op jit(solution)/shard_map/all_gather | solution.py:84
Sparse Core Ops, SparseCore 0:
  9.9 132.9 all-gather.4
  275.3 61.2 all-gather.2
where the time goes:
time: 358 us; the launch traced here: 357 us
  waiting for transfers between devices  211 us (59%)
  matrix products  47.8 us (13%)
  local copies, waits for them, and re-layouts  37.4 us (10%)
  starting transfers between devices  36.2 us (10%)
  between operations  13.6 us (4%)
  other arithmetic  11.1 us (3%)
    all_gather x1, waiting for transfers between devices, per_device(): all_heads = lax.all_gather(attended, 'head', axis=1, tiled=True)  61.4 us
    all_to_all x1, waiting for transfers between devices, per_device(): lax.all_to_all(sent[1], 'frame', split_axis=1, concat_axis=0, tiled=True)  55 us
    all_to_all x1, waiting for transfers between devices, per_device(): lax.all_to_all(sent[0], 'frame', split_axis=1, concat_axis=0, tiled=True)  54.3 us
    all_to_all x1, waiting for transfers between devices, per_device(): lax.all_to_all(sent[2], 'frame', split_axis=1, concat_axis=0, tiled=True)  32 us
    dot_general x1, matrix products, per_device(): jnp.dot(all_heads, lax.all_gather(out_weight, 'frame', axis=0, tiled=True...  13.8 us
    all_to_all x1, starting transfers between devices, per_device(): lax.all_to_all(sent[0], 'frame', split_axis=1, concat_axis=0, tiled=True)  12.1 us
    all_to_all x1, starting transfers between devices, per_device(): lax.all_to_all(sent[1], 'frame', split_axis=1, concat_axis=0, tiled=True)  11.6 us
    sub x1, matrix products, attend_heads(): expo = jnp.exp(scores - largest)  9.79 us
  transfers between devices with their start and end apart: 6, of which 5 were waited for; matrix products, arithmetic and copies ran while one was open for 23% of the time, Pallas kernels for 0%

commit v1 on v0

v1 whole, which is shorter than its diff:
```python
import functools
import math

import jax
import jax.numpy as jnp
from jax import lax
from jax.experimental import pallas as pl
from jax.experimental.pallas import tpu as pltpu
from jax.sharding import PartitionSpec as P

MESH = pl.DeviceIdType.MESH
BF16 = jnp.bfloat16
F32 = jnp.float32
HDIM = 128
POS = 1024
FRAMES = 32
NY, NZ, NX = 4, 8, 4
GROUPS = 8
HEAD_DEV = 5
PB = POS // FRAMES
WROWS = 160
COLS = 640
EXP_SCALE = HDIM**-0.5 * math.log2(math.e)
NEG = -1e30

SLOT_EITHER = 2
SENT = (2, 3, 4)


def wait_on(ref, sem):
    pltpu.make_async_copy(ref, ref, sem).wait()


def remote(src, dst, send_sem, recv_sem, device):
    return pltpu.make_async_remote_copy(
        src_ref=src,
        dst_ref=dst,
        send_sem=send_sem,
        recv_sem=recv_sem,
        device_id=device,
        device_id_type=MESH,
    )


def frame_rows(frame):
    return pl.ds(pl.multiple_of(frame * PB, PB), PB)


def partner(k, y, z):
    turn = (k * 11) % FRAMES
    return ((y + turn // NZ) % NY) * NZ + (z + turn % NZ) % NZ


class WeightRing:
    def __init__(self, rows, zs, zr, ys, yr, head, y, z):
        self.rows, self.zs, self.zr, self.ys, self.yr = rows, zs, zr, ys, yr
        self.y, self.z = y, z
        self.z_next = (y * NZ + (z + 1) % NZ, head)
        self.z_prev = (y * NZ + (z + NZ - 1) % NZ, head)
        self.y_next = (((y + 1) % NY) * NZ + z, head)
        self.y_prev = (((y + NY - 1) % NY) * NZ + z, head)

    def block(self, y, z, half=None):
        row = ((y % NY) * NZ + z % NZ) * WROWS
        if half is None:
            return self.rows.at[pl.ds(row // 16, WROWS // 16)]
        return self.rows.at[pl.ds(row // 16 + half * 5, 5)]

    def send_z(self, t):
        up = self.block(self.y, self.z + NZ + 1 - t, None if t < 4 else 0)
        down = self.block(self.y, self.z + t - 1, None if t < 4 else 1)
        remote(up, up, self.zs.at[0, t - 1], self.zr.at[0, t - 1], self.z_next).start()
        remote(down, down, self.zs.at[1, t - 1], self.zr.at[1, t - 1], self.z_prev).start()

    def wait_z(self, t):
        wait_on(self.block(self.y, self.z + NZ - t, None if t < 4 else 0), self.zr.at[0, t - 1])
        wait_on(self.block(self.y, self.z + t, None if t < 4 else 1), self.zr.at[1, t - 1])

    def send_y(self, dz):
        own = self.block(self.y, self.z + dz)
        remote(own, own, self.ys.at[0, dz], self.yr.at[0, dz], self.y_next).start()
        remote(own, own, self.ys.at[1, dz], self.yr.at[1, dz], self.y_prev).start()

    def relay_y(self, dz):
        wait_on(self.block(self.y + NY - 1, self.z + dz), self.yr.at[0, dz])
        low = self.block(self.y + NY - 1, self.z + dz, 0)
        remote(low, low, self.ys.at[2, dz], self.yr.at[2, dz], self.y_next).start()
        wait_on(self.block(self.y + 1, self.z + dz), self.yr.at[1, dz])
        high = self.block(self.y + 1, self.z + dz, 1)
        remote(high, high, self.ys.at[3, dz], self.yr.at[3, dz], self.y_prev).start()

    def finish_y(self, dz):
        wait_on(self.block(self.y + 2, self.z + dz, 0), self.yr.at[2, dz])
        wait_on(self.block(self.y + 2, self.z + dz, 1), self.yr.at[3, dz])

    def drain(self):
        whole, half = self.block(self.y, self.z), self.block(self.y, self.z, 0)
        for t in range(1, 5):
            for way in range(2):
                wait_on(whole if t < 4 else half, self.zs.at[way, t - 1])
        for dz in range(NZ):
            for way in range(4):
                wait_on(whole if way < 2 else half, self.ys.at[way, dz])


class AttendedRing:
    def __init__(self, groups, send, recv, frame, x, core):
        self.groups, self.send, self.recv = groups, send, recv
        self.x, self.core = x, core
        self.next = (frame, ((x + 1) % NX) * 2 + core)
        self.prev = (frame, ((x + NX - 1) % NX) * 2 + core)
        self.other = (frame, x * 2 + 1 - core)

    def whole(self, x, core):
        return self.groups.at[(x % NX) * 2 + core]

    def half(self, x, core, k):
        return self.groups.at[(x % NX) * 2 + core, pl.ds(k * 512, 512), :]

    def copy(self, ref, k, device):
        remote(ref, ref, self.send.at[k], self.recv.at[k], device).start()

    def own(self):
        mine = self.whole(self.x, self.core)
        self.copy(mine, 0, self.next)
        self.copy(mine, 1, self.prev)
        self.copy(mine, 2, self.other)

    def relay(self):
        came = self.whole(self.x + NX - 1, self.core)
        wait_on(came, self.recv.at[0])
        self.copy(self.half(self.x + NX - 1, self.core, 0), 3, self.next)
        self.copy(came, 5, self.other)
        came = self.whole(self.x + 1, self.core)
        wait_on(came, self.recv.at[1])
        self.copy(self.half(self.x + 1, self.core, 1), 4, self.prev)
        self.copy(came, 6, self.other)

    def relay_far(self):
        for k in range(2):
            came = self.half(self.x + 2, self.core, k)
            wait_on(came, self.recv.at[3 + k])
            self.copy(came, 7 + k, self.other)

    def finish(self):
        across = 1 - self.core
        wait_on(self.whole(self.x, across), self.recv.at[2])
        wait_on(self.whole(self.x + NX - 1, across), self.recv.at[5])
        wait_on(self.whole(self.x + 1, across), self.recv.at[6])
        wait_on(self.half(self.x + 2, across, 0), self.recv.at[7])
        wait_on(self.half(self.x + 2, across, 1), self.recv.at[8])

    def drain(self):
        whole, half = self.whole(self.x, self.core), self.half(self.x, self.core, 0)
        for k in (0, 1, 2, 5, 6):
            wait_on(whole, self.send.at[k])
        for k in (3, 4, 7, 8):
            wait_on(half, self.send.at[k])


def softmax_rows(scores):
    largest = jnp.max(scores, axis=-1, keepdims=True)
    expo = jnp.exp2((scores - largest) * EXP_SCALE)
    return expo.astype(BF16), jnp.sum(expo, axis=-1, keepdims=True)


def dot_t(a, b):
    return lax.dot_general(a, b, (((1,), (1,)), ((), ())), preferred_element_type=F32)


def block_kernel(
    info,
    q_hbm,
    k_hbm,
    v_hbm,
    w_hbm,
    out,
    heads_in,
    slots,
    got,
    mixed,
    either_spatial,
    either_temporal,
    gathered,
    weight,
    picked_weight,
    total,
    load_sem,
    fwd_send,
    fwd_recv,
    ret_send,
    ret_recv,
    wz_send,
    wz_recv,
    wy_send,
    wy_recv,
    x_send,
    x_recv,
):
    frame, head = lax.axis_index("frame"), lax.axis_index("head")
    y, z = frame // NZ, frame % NZ
    x, core = head // 2, head % 2

    loads = [
        pltpu.make_async_copy(
            source.at[:, pl.ds(h * HDIM, HDIM)], heads_in.at[n, h], load_sem.at[n, h]
        )
        for n, source in enumerate((q_hbm, k_hbm, v_hbm))
        for h in range(HEAD_DEV)
    ]
    loads += [
        pltpu.make_async_copy(
            w_hbm.at[pl.ds(n * 16, 16), :], weight.at[frame * 10 + n], load_sem.at[3, n]
        )
        for n in range(10)
    ]
    for load in loads:
        load.start()

    barrier = pltpu.get_barrier_semaphore()

    def greet(k, carry):
        pl.semaphore_signal(
            barrier, inc=1, device_id=((frame + k) % FRAMES, head), device_id_type=MESH
        )
        return carry

    lax.fori_loop(1, FRAMES, greet, 0)
    for there in (((x + 1) % NX) * 2 + core, ((x + NX - 1) % NX) * 2 + core, x * 2 + 1 - core):
        pl.semaphore_signal(barrier, inc=1, device_id=(frame, there), device_id_type=MESH)

    for load in loads:
        load.wait()
    for slot in range(HEAD_DEV):
        for n in range(3):
            slots[slot, n] = heads_in[n, info[head * 8 + slot]]

    pl.semaphore_wait(barrier, FRAMES - 1 + 3)

    ring = WeightRing(weight, wz_send, wz_recv, wy_send, wy_recv, head, y, z)
    gather = [
        AttendedRing(gathered.at[slot], x_send.at[slot], x_recv.at[slot], frame, x, core)
        for slot in range(HEAD_DEV)
    ]

    def send_forward(s):
        def one(k, carry):
            to = partner(k, y, z)
            remote(
                slots.at[SENT[s], :, frame_rows(to), :],
                got.at[s, :, frame_rows(frame), :],
                fwd_send.at[s],
                fwd_recv.at[s],
                (to, head),
            ).start()
            return carry

        lax.fori_loop(1, FRAMES, one, 0)
        pltpu.make_async_copy(
            slots.at[SENT[s], :, frame_rows(frame), :],
            got.at[s, :, frame_rows(frame), :],
            fwd_recv.at[s],
        ).start()

    def returned(s):
        return either_temporal if SENT[s] == SLOT_EITHER else gathered.at[SENT[s], head]

    def send_back(s):
        def one(k, carry):
            to = partner(k, y, z)
            remote(
                mixed.at[s, frame_rows(to), :],
                returned(s).at[frame_rows(frame), :],
                ret_send.at[s],
                ret_recv.at[s],
                (to, head),
            ).start()
            return carry

        lax.fori_loop(1, FRAMES, one, 0)
        pltpu.make_async_copy(
            mixed.at[s, frame_rows(frame), :],
            returned(s).at[frame_rows(frame), :],
            ret_recv.at[s],
        ).start()

    def spatial(slot, dest):
        def one(i, carry):
            rows = pl.ds(pl.multiple_of(i * 256, 256), 256)
            expo, row_sum = softmax_rows(dot_t(slots[slot, 0, rows, :], slots[slot, 1]))
            mix = jnp.dot(expo, slots[slot, 2], preferred_element_type=F32)
            dest[rows, :] = (mix / row_sum).astype(BF16)
            return carry

        lax.fori_loop(0, POS // 256, one, 0)

    def temporal(s):
        wait_on(got.at[s], fwd_recv.at[s])
        row_at = lax.broadcasted_iota(jnp.int32, (512, 512), 0) % 16
        col_at = lax.broadcasted_iota(jnp.int32, (512, 512), 1) % 16
        same = row_at == col_at
        for half in range(2):
            query, key, value = (
                got[s, n].reshape(FRAMES, 2, 16, HDIM)[:, half].reshape(512, HDIM)
                for n in range(3)
            )
            expo, row_sum = softmax_rows(jnp.where(same, dot_t(query, key), NEG))
            mix = jnp.dot(expo, value, preferred_element_type=F32)
            mix = (mix / row_sum).astype(BF16).reshape(FRAMES, 16, HDIM)
            for f in range(FRAMES):
                mixed[s, pl.ds(f * PB + half * 16, 16), :] = mix[f]

    def project(slot, first, last):
        for g in range(GROUPS):
            at = (info[g * 8 + slot] + g * HEAD_DEV) * 8
            for n in range(8):
                picked_weight[pl.ds(g * HDIM + n * 16, 16), :] = weight[at + n]

        def one(i, carry):
            rows = pl.ds(pl.multiple_of(i * 256, 256), 256)
            left = jnp.concatenate([gathered[slot, g, rows, :] for g in range(GROUPS)], axis=1)
            part = jnp.dot(left, picked_weight[...], preferred_element_type=F32)
            if not first:
                part = part + total[rows, :]
            if last:
                out[rows, :] = part.astype(BF16)
            else:
                total[rows, :] = part
            return carry

        lax.fori_loop(0, POS // 256, one, 0)

    ring.send_z(1)
    ring.send_y(0)
    send_forward(0)
    spatial(0, gathered.at[0, head])
    gather[0].own()
    ring.wait_z(1)
    ring.send_z(2)
    ring.send_y(1)
    ring.send_y(7)
    send_forward(1)
    spatial(1, gathered.at[1, head])
    gather[1].own()
    ring.wait_z(2)
    ring.send_z(3)
    ring.send_y(2)
    ring.send_y(6)
    ring.relay_y(0)
    send_forward(2)
    spatial(SLOT_EITHER, either_spatial)
    gather[0].relay()
    ring.wait_z(3)
    ring.send_z(4)
    ring.send_y(3)
    ring.send_y(5)
    ring.relay_y(1)
    ring.relay_y(7)
    gather[0].relay_far()
    temporal(0)
    send_back(0)
    ring.wait_z(4)
    ring.send_y(4)
    ring.relay_y(2)
    ring.relay_y(6)
    gather[1].relay()
    gather[1].relay_far()
    temporal(1)
    send_back(1)
    ring.relay_y(3)
    ring.relay_y(5)

    wait_on(either_temporal, ret_recv.at[0])
    is_temporal = jnp.full((POS, HDIM), info[head * 8 + HEAD_DEV], jnp.int32) == 1
    gathered[SLOT_EITHER, head] = jnp.where(
        is_temporal, either_temporal[...], either_spatial[...]
    )
    gather[2].own()
    temporal(2)
    send_back(2)
    ring.relay_y(4)
    wait_on(returned(1), ret_recv.at[1])
    gather[3].own()
    gather[2].relay()
    gather[2].relay_far()
    for dz in range(NZ):
        ring.finish_y(dz)
    gather[0].finish()
    project(0, True, False)
    gather[3].relay()
    wait_on(returned(2), ret_recv.at[2])
    gather[4].own()
    gather[3].relay_far()
    gather[1].finish()
    project(1, False, False)
    gather[4].relay()
    gather[2].finish()
    project(2, False, False)
    gather[4].relay_far()
    gather[3].finish()
    project(3, False, False)
    gather[4].finish()
    project(4, False, True)

    ring.drain()
    for each in gather:
        each.drain()
    for s in range(3):
        wait_on(slots.at[SENT[s], :, pl.ds(0, POS - PB), :], fwd_send.at[s])
        wait_on(mixed.at[s, pl.ds(0, POS - PB), :], ret_send.at[s])


def slot_table(head_labels):
    labels = head_labels.reshape(GROUPS, HEAD_DEV)
    spatial = 1 - labels
    n_spatial = jnp.sum(spatial, axis=1, keepdims=True)
    rank = jnp.where(
        labels == 0,
        jnp.cumsum(spatial, axis=1) - 1,
        n_spatial + jnp.cumsum(labels, axis=1) - 1,
    )
    at = jnp.arange(HEAD_DEV, dtype=jnp.int32)
    heads = jnp.sum(jnp.where(rank[:, :, None] == at, at[None, :, None], 0), axis=1)
    table = jnp.concatenate(
        [heads, (n_spatial == 2).astype(jnp.int32), jnp.zeros((GROUPS, 2), jnp.int32)], axis=1
    )
    return table.reshape(GROUPS * 8)


def per_device(queries, key_states, value_states, out_weight, head_labels):
    any_spec = pl.BlockSpec(memory_space=pl.ANY)
    dma = pltpu.SemaphoreType.DMA
    return pl.pallas_call(
        block_kernel,
        out_shape=jax.ShapeDtypeStruct((POS, COLS), BF16),
        in_specs=[pl.BlockSpec(memory_space=pltpu.SMEM)] + [any_spec] * 4,
        out_specs=pl.BlockSpec(memory_space=pltpu.VMEM),
        scratch_shapes=[
            pltpu.VMEM((3, HEAD_DEV, POS, HDIM), BF16),
            pltpu.VMEM((HEAD_DEV, 3, POS, HDIM), BF16),
            pltpu.VMEM((3, 3, POS, HDIM), BF16),
            pltpu.VMEM((3, POS, HDIM), BF16),
            pltpu.VMEM((POS, HDIM), BF16),
            pltpu.VMEM((POS, HDIM), BF16),
            pltpu.VMEM((HEAD_DEV, GROUPS, POS, HDIM), BF16),
            pltpu.VMEM((WROWS * FRAMES // 16, 16, COLS), BF16),
            pltpu.VMEM((GROUPS * HDIM, COLS), BF16),
            pltpu.VMEM((POS, COLS), F32),
            dma((4, 10)),
            dma((3,)),
            dma((3,)),
            dma((3,)),
            dma((3,)),
            dma((2, 4)),
            dma((2, 4)),
            dma((4, NZ)),
            dma((4, NZ)),
            dma((HEAD_DEV, 9)),
            dma((HEAD_DEV, 9)),
        ],
        compiler_params=pltpu.CompilerParams(
            collective_id=0, has_side_effects=True, vmem_limit_bytes=56 << 20
        ),
        name="block_kernel",
    )(slot_table(head_labels), queries, key_states, value_states, out_weight)


def solution(mesh):
    return jax.shard_map(
        per_device,
        mesh=mesh,
        in_specs=(
            P("frame", "head"),
            P("frame", "head"),
            P("frame", "head"),
            P("frame", "head"),
            P(),
        ),
        out_specs=P("frame", "head"),
        check_vma=False,
    )
```

time: 358 us -> 135 us (0.38)
  waiting for transfers between devices: 211 us -> 0 us
  Pallas kernels: 0 us -> 130 us
  matrix products: 47.8 us -> 0 us
  starting transfers between devices: 36.2 us -> 0 us
  local copies, waits for them, and re-layouts: 37.4 us -> 4.06 us
  between operations: 13.6 us -> 0.02 us
  other arithmetic: 11.1 us -> 0.66 us
    all_to_all x4 -> x0, waiting for transfers between devices: 149 us -> none  [the longest x1 55 us: per_device(): lax.all_to_all(sent[1], 'frame', split_axis=1, concat_axis=0, tiled=True)]
    pallas_call x0 -> x1, Pallas kernels: none -> 130 us  [per_device(): pl.pallas_call(block_kernel, out_shape=jax.ShapeDtypeStruct((POS, COLS),...]
    all_gather x2 -> x0, waiting for transfers between devices: 61.4 us -> none  [the longest x1 61.4 us: per_device(): all_heads = lax.all_gather(attended, 'head', axis=1, tiled=True)]
    dot_general x6 -> x0, matrix products: 38 us -> none  [the longest x1 13.8 us: per_device(): jnp.dot(all_heads, lax.all_gather(out_weight, 'frame', axis=0, tiled=True...]
    all_to_all x4 -> x0, starting transfers between devices: 36.2 us -> none  [the longest x1 12.1 us: per_device(): lax.all_to_all(sent[0], 'frame', split_axis=1, concat_axis=0, tiled=True)]
    gather x8 -> x0, local copies, waits for them, and re-layouts: 12 us -> none  [the longest x1 3.16 us: per_device(): jnp.take(value_per_head, picked, axis=1)[None]]
    sub x1 -> x0, matrix products: 9.79 us -> none  [attend_heads(): expo = jnp.exp(scores - largest)]
    broadcast_in_dim x3 -> x0, local copies, waits for them, and re-layouts: 9.45 us -> none  [the longest x1 3.61 us: per_device(): jnp.take(key_heads, picked, axis=1)[None]]
  transfers between devices with their start and end apart: 6 -> 0, of which waited for: 5 -> 0; matrix products, arithmetic and copies ran while one was open for 23% -> 0% of each run, Pallas kernels for 0% -> 0%
where the time goes in v1:
time: 135 us
  Pallas kernels  130 us (96%)
  local copies, waits for them, and re-layouts  4.06 us (3%)
    pallas_call x1, Pallas kernels, per_device(): pl.pallas_call(block_kernel, out_shape=jax.ShapeDtypeStruct((POS, COLS),...  130 us

profile of v1, /device:TPU:1, one launch (start us, length us, event | category | flops | bytes accessed | tf_op | source)
XLA Modules:
  0.0 134.7 jit_solution(10643756326970262102)
XLA Ops:
  0.0 0.1 pad.2.clone
  0.1 0.7 reshape.63
  0.8 0.2 reduce_window_sum.18
  1.0 0.1 broadcast_subtract_fusion
  1.1 0.2 reduce_window_sum.17
  1.2 0.1 add_select_fusion
  1.3 0.1 copy.7
  1.4 0.1 select_reduce_fusion
  1.5 0.1 copy.8
  1.6 0.1 add_add_fusion
  1.6 0.6 reshape.64.info
  2.2 130.0 %block_kernel.1 = bf16[1024,640]{1,0:T(8,128)(2,1)} custom-call(s32[64]{0:T(128)} %reshape.64.info, bf16[1024,640]{1,0:T(8,128)(2,1)} %q_hbm.1, bf16[1024,640]{1,0:T(8,128)(2,1)} %k_hbm.1, bf16[1024,640]{1,0:T(8,128)(2,1)} %v_hbm.1, bf16[160,640]{1,0:T(8,128)(2,1)} %w_hbm.1), custom_call_target="tpu_custom_call" | custom-call | tf_op jit(solution)/shard_map/block_kernel/pallas_call | solution.py:433
  132.2 2.5 %copy.10 = bf16[1024,640]{1,0:T(8,128)(2,1)} copy(bf16[1024,640]{1,0:T(8,128)(2,1)} %block_kernel.1) | data formatting | bytes 2621440
  (2 shorter events, 0.0 us)

commit v2 on v1

v2 whole, which is shorter than its diff:
```python
import functools
import math

import jax
import jax.numpy as jnp
from jax import lax
from jax.experimental import pallas as pl
from jax.experimental.pallas import tpu as pltpu
from jax.sharding import PartitionSpec as P

MESH = pl.DeviceIdType.MESH
BF16 = jnp.bfloat16
F32 = jnp.float32
HDIM = 128
POS = 1024
FRAMES = 32
NY, NZ, NX = 4, 8, 4
GROUPS = 8
HEAD_DEV = 5
PB = POS // FRAMES
WROWS = 160
COLS = 640
EXP_SCALE = HDIM**-0.5 * math.log2(math.e)
NEG = -1e30
HALF = PB // 2
TILED = (FRAMES, 2, HALF, HDIM)

SLOT_EITHER = 2
SENT = (2, 3, 4)

ORDER = (
    ("zs", 1), ("ys", 0), ("pick", 2), ("fwd", 0, 0), ("fwd", 0, 1), ("pick", 0), ("pick", 1), ("pick", 3),
    ("pick", 4), ("zw", 1), ("zs", 2), ("ys", 1), ("ys", 7), ("fwd", 0, 2), ("fwd", 0, 3), ("sp", 0),
    ("xo", 0), ("yr", 0), ("zw", 2), ("ys", 2), ("ys", 6), ("fwd", 1, 0), ("fwd", 1, 1), ("zs", 3),
    ("fwd", 1, 2), ("fwd", 1, 3), ("sp", 1), ("xo", 1), ("yr", 1), ("yr", 7), ("tm", 0), ("sp", 2), ("xr", 0),
    ("xf", 0), ("yr", 2), ("yr", 6), ("zw", 3), ("zs", 4), ("ys", 3), ("ys", 5), ("fwh", 0, 0), ("back", 0),
    ("xo", 2), ("xr", 1), ("xf", 1), ("tm", 1), ("fwh", 0, 1), ("xr", 2), ("zw", 4), ("ys", 4), ("fwh", 1, 0),
    ("fwh", 1, 1), ("yr", 3), ("yr", 5), ("xf", 2), ("xe", 0), ("xe", 1), ("mm", 0), ("xe", 2), ("back", 1),
    ("xo", 3), ("yr", 4), ("mm", 1), ("tmh", 0), ("xr", 3), ("mm", 2), ("tmh", 1), ("mm", 3), ("xf", 3),
    ("bkh", 0), ("xo", 4), ("ye", 0), ("ye", 1), ("ye", 7), ("ye", 2), ("ye", 6), ("ye", 3), ("ye", 5),
    ("ye", 4), ("mm", 4), ("bkh", 1), ("xo", 5), ("xe", 3), ("xr", 4), ("mm", 5, 0), ("xr", 5), ("mm", 5, 1),
    ("xf", 4), ("xf", 5), ("xe", 4), ("mm", 6, 0), ("xe", 5), ("mm", 6, 1),
)


UNITS = (
    ((0, 1), (0,)),
    ((0, 1), (1,)),
    ((0, 1), (3,)),
    ((2,), (0, 1, 3)),
    ((0, 1, 2), (2,)),
    ((3,), (0, 1, 2, 3)),
    ((4,), (0, 1, 2, 3)),
)


def wait_on(ref, sem):
    pltpu.make_async_copy(ref, ref, sem).wait()


def remote(src, dst, send_sem, recv_sem, device):
    return pltpu.make_async_remote_copy(
        src_ref=src,
        dst_ref=dst,
        send_sem=send_sem,
        recv_sem=recv_sem,
        device_id=device,
        device_id_type=MESH,
    )


def partner(k, y, z):
    turn = (k * 11) % FRAMES
    return ((y + turn // NZ) % NY) * NZ + (z + turn % NZ) % NZ


class WeightRing:
    def __init__(self, rows, zs, zr, ys, yr, head, y, z):
        self.rows, self.zs, self.zr, self.ys, self.yr = rows, zs, zr, ys, yr
        self.z = z
        self.z_next = (y * NZ + (z + 1) % NZ, head)
        self.z_prev = (y * NZ + (z + NZ - 1) % NZ, head)
        self.y_next = (((y + 1) % NY) * NZ + z, head)
        self.y_prev = (((y + NY - 1) % NY) * NZ + z, head)

    def block(self, d, dz, half=None):
        unit = ((self.z + dz) % NZ) * 10
        if half is None:
            return self.rows[d].at[pl.ds(unit, 10)]
        return self.rows[d].at[pl.ds(unit + half * 5, 5)]

    def send_z(self, t):
        up = self.block(0, NZ + 1 - t, None if t < 4 else 0)
        down = self.block(0, t - 1, None if t < 4 else 1)
        remote(up, up, self.zs.at[0, t - 1], self.zr.at[0, t - 1], self.z_next).start()
        remote(down, down, self.zs.at[1, t - 1], self.zr.at[1, t - 1], self.z_prev).start()

    def wait_z(self, t):
        wait_on(self.block(0, NZ - t, None if t < 4 else 0), self.zr.at[0, t - 1])
        wait_on(self.block(0, t, None if t < 4 else 1), self.zr.at[1, t - 1])

    def send_y(self, dz):
        own = self.block(0, dz)
        remote(own, self.block(3, dz), self.ys.at[0, dz], self.yr.at[0, dz], self.y_next).start()
        remote(own, self.block(1, dz), self.ys.at[1, dz], self.yr.at[1, dz], self.y_prev).start()

    def relay_y(self, dz):
        for way, d, to in ((0, 3, self.y_next), (1, 1, self.y_prev)):
            wait_on(self.block(d, dz), self.yr.at[way, dz])
            remote(
                self.block(d, dz, way),
                self.block(2, dz, way),
                self.ys.at[2 + way, dz],
                self.yr.at[2 + way, dz],
                to,
            ).start()

    def finish_y(self, dz):
        for way in range(2):
            wait_on(self.block(2, dz, way), self.yr.at[2 + way, dz])

    def drain(self):
        whole, half = self.block(0, 0), self.block(0, 0, 0)
        for t in range(1, 5):
            for way in range(2):
                wait_on(whole if t < 4 else half, self.zs.at[way, t - 1])
        for dz in range(NZ):
            for way in range(4):
                wait_on(whole if way < 2 else half, self.ys.at[way, dz])


class AttendedRing:
    def __init__(self, groups, send, recv, frame, x, core):
        self.groups, self.send, self.recv = groups, send, recv
        self.x, self.core = x, core
        self.next = (frame, ((x + 1) % NX) * 2 + core)
        self.prev = (frame, ((x + NX - 1) % NX) * 2 + core)
        self.other = (frame, x * 2 + 1 - core)

    def whole(self, x, core):
        return self.groups.at[(x % NX) * 2 + core]

    def half(self, x, core, k):
        return self.groups.at[(x % NX) * 2 + core, pl.ds(k * (FRAMES // 2), FRAMES // 2)]

    def copy(self, ref, k, device):
        remote(ref, ref, self.send.at[k], self.recv.at[k], device).start()

    def own(self):
        mine = self.whole(self.x, self.core)
        self.copy(mine, 0, self.next)
        self.copy(mine, 1, self.prev)
        self.copy(mine, 2, self.other)

    def relay(self):
        came = self.whole(self.x + NX - 1, self.core)
        wait_on(came, self.recv.at[0])
        self.copy(self.half(self.x + NX - 1, self.core, 0), 3, self.next)
        self.copy(came, 5, self.other)
        came = self.whole(self.x + 1, self.core)
        wait_on(came, self.recv.at[1])
        self.copy(self.half(self.x + 1, self.core, 1), 4, self.prev)
        self.copy(came, 6, self.other)

    def relay_far(self):
        for k in range(2):
            came = self.half(self.x + 2, self.core, k)
            wait_on(came, self.recv.at[3 + k])
            self.copy(came, 7 + k, self.other)

    def finish(self):
        across = 1 - self.core
        wait_on(self.whole(self.x, across), self.recv.at[2])
        wait_on(self.whole(self.x + NX - 1, across), self.recv.at[5])
        wait_on(self.whole(self.x + 1, across), self.recv.at[6])
        wait_on(self.half(self.x + 2, across, 0), self.recv.at[7])
        wait_on(self.half(self.x + 2, across, 1), self.recv.at[8])

    def drain(self):
        whole, half = self.whole(self.x, self.core), self.half(self.x, self.core, 0)
        for k in (0, 1, 2, 5, 6):
            wait_on(whole, self.send.at[k])
        for k in (3, 4, 7, 8):
            wait_on(half, self.send.at[k])


def softmax_rows(scores):
    largest = jnp.max(scores, axis=-1, keepdims=True)
    expo = jnp.exp2((scores - largest) * EXP_SCALE)
    return expo.astype(BF16), jnp.sum(expo, axis=-1, keepdims=True)


def dot_t(a, b):
    return lax.dot_general(a, b, (((1,), (1,)), ((), ())), preferred_element_type=F32)


def block_kernel(
    labels,
    q_hbm,
    k_hbm,
    v_hbm,
    w_hbm,
    out,
    table,
    heads_in,
    slots,
    got,
    mixed,
    either_spatial,
    either_temporal,
    gathered,
    weight0,
    weight1,
    weight2,
    weight3,
    picked_weight,
    total,
    result,
    load_sem,
    out_sem,
    fwd_send,
    fwd_recv,
    ret_send,
    ret_recv,
    wz_send,
    wz_recv,
    wy_send,
    wy_recv,
    x_send,
    x_recv,
):
    frame, head = lax.axis_index("frame"), lax.axis_index("head")
    y, z = frame // NZ, frame % NZ
    weight = (weight0, weight1, weight2, weight3)
    x, core = head // 2, head % 2

    loads = [
        pltpu.make_async_copy(
            w_hbm.at[pl.ds(n * 16, 16), :], weight0.at[z * 10 + n], load_sem.at[3, n]
        )
        for n in range(10)
    ]
    loads += [
        pltpu.make_async_copy(
            source.at[:, pl.ds(h * HDIM, HDIM)], heads_in.at[n, h], load_sem.at[n, h]
        )
        for n, source in enumerate((q_hbm, k_hbm, v_hbm))
        for h in range(HEAD_DEV)
    ]
    for load in loads:
        load.start()

    barrier = pltpu.get_barrier_semaphore()

    def greet(k, carry):
        pl.semaphore_signal(
            barrier, inc=1, device_id=((frame + k) % FRAMES, head), device_id_type=MESH
        )
        return carry

    lax.fori_loop(1, FRAMES, greet, 0)
    for there in (((x + 1) % NX) * 2 + core, ((x + NX - 1) % NX) * 2 + core, x * 2 + 1 - core):
        pl.semaphore_signal(barrier, inc=1, device_id=(frame, there), device_id_type=MESH)

    def fill(g, line):
        label = [labels[g * HEAD_DEV + h] for h in range(HEAD_DEV)]
        temporal_count = sum(label)
        rank, ones = [], 0
        for h in range(HEAD_DEV):
            rank.append(label[h] * (HEAD_DEV - temporal_count + ones) + (1 - label[h]) * (h - ones))
            ones = ones + label[h]
        for slot in range(HEAD_DEV):
            table[line * 8 + slot] = sum(
                h * (rank[h] == slot).astype(jnp.int32) for h in range(HEAD_DEV)
            )
        table[line * 8 + HEAD_DEV] = temporal_count - 2

    fill(head, 0)
    for g in range(GROUPS):
        fill(g, 1 + g)

    def pick(slot):
        if slot == SLOT_EITHER:
            for load in loads[10:]:
                load.wait()
        for n in range(3):
            slots[slot, n] = heads_in[n, table[slot]].reshape(TILED)

    for load in loads[:10]:
        load.wait()
    pl.semaphore_wait(barrier, FRAMES - 1 + 3)

    ring = WeightRing(weight, wz_send, wz_recv, wy_send, wy_recv, head, y, z)
    gather = [
        AttendedRing(ref, x_send.at[n], x_recv.at[n], frame, x, core)
        for n, ref in enumerate(
            [gathered.at[slot] for slot in range(4)] + [gathered.at[4, :, :, h] for h in range(2)]
        )
    ]

    def send_forward(sem, first, last, source, target):
        def one(k, carry):
            to = partner(k, y, z)
            remote(
                source(to), target(frame), fwd_send.at[sem], fwd_recv.at[sem], (to, head)
            ).start()
            return carry

        lax.fori_loop(first, last, one, 0)
        if first == 1:
            pltpu.make_async_copy(source(frame), target(frame), fwd_recv.at[sem]).start()

    def forward(s, part):
        send_forward(
            s,
            max(1, part * 8),
            part * 8 + 8,
            lambda to: slots.at[SENT[s], :, to],
            lambda here: got.at[s, :, here],
        )

    def forward_half(h, part):
        send_forward(
            2 + h,
            max(1, part * 16),
            part * 16 + 16,
            lambda to: slots.at[4, :, to, h],
            lambda here: got.at[2, :, here, h],
        )

    def returned(s):
        return either_temporal if SENT[s] == SLOT_EITHER else gathered.at[SENT[s], head]

    def send_back(sem, source, target):
        def one(k, carry):
            to = partner(k, y, z)
            remote(
                source(to), target(frame), ret_send.at[sem], ret_recv.at[sem], (to, head)
            ).start()
            return carry

        lax.fori_loop(1, FRAMES, one, 0)
        pltpu.make_async_copy(source(frame), target(frame), ret_recv.at[sem]).start()

    def spatial(slot):
        def one(i, carry):
            blocks = pl.ds(i * 8, 8)
            query = slots[slot, 0, blocks].reshape(256, HDIM)
            key, value = (slots[slot, n].reshape(POS, HDIM) for n in (1, 2))
            expo, row_sum = softmax_rows(dot_t(query, key))
            mix = jnp.dot(expo, value, preferred_element_type=F32)
            mix = (mix / row_sum).astype(BF16).reshape(8, 2, HALF, HDIM)
            if slot == SLOT_EITHER:
                either_spatial[blocks] = mix
            else:
                gathered[slot, head, blocks] = mix
            return carry

        lax.fori_loop(0, POS // 256, one, 0)

    def temporal(s, h):
        rows = FRAMES * HALF
        row_at = lax.broadcasted_iota(jnp.int32, (rows, rows), 0) % HALF
        col_at = lax.broadcasted_iota(jnp.int32, (rows, rows), 1) % HALF
        query, key, value = (got[s, n, :, h].reshape(rows, HDIM) for n in range(3))
        expo, row_sum = softmax_rows(jnp.where(row_at == col_at, dot_t(query, key), NEG))
        mix = jnp.dot(expo, value, preferred_element_type=F32)
        mixed[s, :, h] = (mix / row_sum).astype(BF16).reshape(FRAMES, HALF, HDIM)

    def attend_temporal(s):
        wait_on(got.at[s], fwd_recv.at[s])
        for h in range(2):
            temporal(s, h)
        send_back(s, lambda to: mixed.at[s, to], lambda here: returned(s).at[here])

    def attend_temporal_half(h):
        wait_on(got.at[2, :, :, h], fwd_recv.at[2 + h])
        temporal(2, h)
        send_back(
            2 + h, lambda to: mixed.at[2, to, h], lambda here: gathered.at[4, head, here, h]
        )

    def come_back(s):
        wait_on(returned(s), ret_recv.at[s])
        if SENT[s] == SLOT_EITHER:
            is_temporal = jnp.full(TILED, table[HEAD_DEV], jnp.int32) == 1
            gathered[SLOT_EITHER, head] = jnp.where(
                is_temporal, either_temporal[...], either_spatial[...]
            )

    def come_back_half(h):
        wait_on(gathered.at[4, head, :, h], ret_recv.at[2 + h])

    def groups_at(d):
        there = (y + d) % NY
        return [(there * 2 + c, c) for c in range(2)]

    def pick_weight(picks):
        for n, (slot, d, g, c) in enumerate(picks):
            at = (table[(1 + g) * 8 + slot] + c * HEAD_DEV) * 8
            for m in range(8):
                picked_weight[pl.ds(n * HDIM + m * 16, 16), :] = weight[d][at + m]

    def project(unit, part=None):
        taken, offsets = UNITS[unit]
        picks = [(slot, d, g, c) for slot in taken for d in offsets for g, c in groups_at(d)]
        depth = len(picks) * HDIM
        if part != 1:
            pick_weight(picks)

        def one(i, carry):
            at = (pl.ds(i * 8, 8),) if part is None else (pl.ds(i * 16, 16), part)
            left = jnp.concatenate(
                [gathered[(slot, g) + at].reshape(256, HDIM) for slot, d, g, c in picks], axis=1
            )
            sums = jnp.dot(left, picked_weight[:depth, :], preferred_element_type=F32)
            sums = sums.reshape(total[at].shape)
            if unit != 0:
                sums = sums + total[at]
            if taken == (4,):
                result[at] = sums.astype(BF16)
            else:
                total[at] = sums
            return carry

        lax.fori_loop(0, 4 if part is None else 2, one, 0)
        if taken == (4,):
            store(part).start()

    def store(h):
        return pltpu.make_async_copy(result.at[:, h], out.at[:, h], out_sem.at[h])

    acts = {
        "pick": pick,
        "zs": ring.send_z,
        "zw": ring.wait_z,
        "ys": ring.send_y,
        "yr": ring.relay_y,
        "ye": ring.finish_y,
        "fwd": forward,
        "fwh": forward_half,
        "sp": spatial,
        "tm": attend_temporal,
        "tmh": attend_temporal_half,
        "back": come_back,
        "bkh": come_back_half,
        "xo": lambda n: gather[n].own(),
        "xr": lambda n: gather[n].relay(),
        "xf": lambda n: gather[n].relay_far(),
        "xe": lambda n: gather[n].finish(),
        "mm": project,
    }
    for act, *at in ORDER:
        acts[act](*at)

    for h in range(2):
        store(h).wait()
    ring.drain()
    for each in gather:
        each.drain()
    for s in range(2):
        wait_on(slots.at[SENT[s], :, pl.ds(0, FRAMES - 1)], fwd_send.at[s])
        wait_on(mixed.at[s, pl.ds(0, FRAMES - 1)], ret_send.at[s])
    for h in range(2):
        wait_on(slots.at[4, :, pl.ds(0, FRAMES - 1), h], fwd_send.at[2 + h])
        wait_on(mixed.at[2, pl.ds(0, FRAMES - 1), h], ret_send.at[2 + h])


def per_device(queries, key_states, value_states, out_weight, head_labels):
    any_spec = pl.BlockSpec(memory_space=pl.ANY)
    dma = pltpu.SemaphoreType.DMA
    return pl.pallas_call(
        block_kernel,
        out_shape=pltpu.VMEM((FRAMES, 2, HALF, COLS), BF16),
        in_specs=[pl.BlockSpec(memory_space=pltpu.SMEM)] + [any_spec] * 4,
        out_specs=any_spec,
        scratch_shapes=[
            pltpu.SMEM(((1 + GROUPS) * 8,), jnp.int32),
            pltpu.VMEM((3, HEAD_DEV, POS, HDIM), BF16),
            pltpu.VMEM((HEAD_DEV, 3) + TILED, BF16),
            pltpu.VMEM((3, 3) + TILED, BF16),
            pltpu.VMEM((3,) + TILED, BF16),
            pltpu.VMEM(TILED, BF16),
            pltpu.VMEM(TILED, BF16),
            pltpu.VMEM((HEAD_DEV, GROUPS) + TILED, BF16),
            pltpu.VMEM((WROWS * NZ // 16, 16, COLS), BF16),
            pltpu.VMEM((WROWS * NZ // 16, 16, COLS), BF16),
            pltpu.VMEM((WROWS * NZ // 16, 16, COLS), BF16),
            pltpu.VMEM((WROWS * NZ // 16, 16, COLS), BF16),
            pltpu.VMEM((GROUPS * HDIM, COLS), BF16),
            pltpu.VMEM((FRAMES, 2, HALF, COLS), F32),
            pltpu.VMEM((FRAMES, 2, HALF, COLS), BF16),
            dma((4, 10)),
            dma((2,)),
            dma((4,)),
            dma((4,)),
            dma((4,)),
            dma((4,)),
            dma((2, 4)),
            dma((2, 4)),
            dma((4, NZ)),
            dma((4, NZ)),
            dma((HEAD_DEV + 1, 9)),
            dma((HEAD_DEV + 1, 9)),
        ],
        compiler_params=pltpu.CompilerParams(
            collective_id=0, has_side_effects=True, vmem_limit_bytes=56 << 20
        ),
        name="block_kernel",
    )(head_labels, queries, key_states, value_states, out_weight).reshape(POS, COLS)


def solution(mesh):
    return jax.shard_map(
        per_device,
        mesh=mesh,
        in_specs=(
            P("frame", "head"),
            P("frame", "head"),
            P("frame", "head"),
            P("frame", "head"),
            P(),
        ),
        out_specs=P("frame", "head"),
        check_vma=False,
    )
```

time: 135 us -> 119 us (0.88)
  Pallas kernels: 130 us -> 118 us
  local copies, waits for them, and re-layouts: 4.06 us -> 1.06 us
    pallas_call x1, Pallas kernels: 130 us -> 118 us  [per_device(): pl.pallas_call(block_kernel, out_shape=pltpu.VMEM((FRAMES, 2, HALF, COLS)...]
    unnamed x1, local copies, waits for them, and re-layouts: 2.49 us -> 1.06 us
where the time goes in v2:
time: 119 us
  Pallas kernels  118 us (99%)
    pallas_call x1, Pallas kernels, per_device(): pl.pallas_call(block_kernel, out_shape=pltpu.VMEM((FRAMES, 2, HALF, COLS)...  118 us

profile of v2, /device:TPU:1, one launch (start us, length us, event | category | flops | bytes accessed | tf_op | source)
XLA Modules:
  0.0 119.2 jit_solution(5254603859663069846)
XLA Ops:
  0.0 118.1 %block_kernel.1 = bf16[32,2,16,640]{3,2,1,0:T(8,128)(2,1)S(1)} custom-call(s32[40]{0:T(128)} %labels.1, bf16[1024,640]{1,0:T(8,128)(2,1)} %q_hbm.1, bf16[1024,640]{1,0:T(8,128)(2,1)} %k_hbm.1, bf16[1024,640]{1,0:T(8,128)(2,1)} %v_hbm.1, bf16[160,640]{1,0:T(8,128)(2,1)} %w_hbm.1), custom_call_target="tpu_custom_call" | custom-call | tf_op jit(solution)/shard_map/block_kernel/pallas_call | solution.py:472
  118.1 1.1 copy.7

commit v3 on v2

--- a/solution.py
+++ b/solution.py
@@ -30,16 +30,16 @@
 
 ORDER = (
     ("zs", 1), ("ys", 0), ("pick", 2), ("fwd", 0, 0), ("fwd", 0, 1), ("pick", 0), ("pick", 1), ("pick", 3),
-    ("pick", 4), ("zw", 1), ("zs", 2), ("ys", 1), ("ys", 7), ("fwd", 0, 2), ("fwd", 0, 3), ("sp", 0),
-    ("xo", 0), ("yr", 0), ("zw", 2), ("ys", 2), ("ys", 6), ("fwd", 1, 0), ("fwd", 1, 1), ("zs", 3),
-    ("fwd", 1, 2), ("fwd", 1, 3), ("sp", 1), ("xo", 1), ("yr", 1), ("yr", 7), ("tm", 0), ("sp", 2), ("xr", 0),
-    ("xf", 0), ("yr", 2), ("yr", 6), ("zw", 3), ("zs", 4), ("ys", 3), ("ys", 5), ("fwh", 0, 0), ("back", 0),
-    ("xo", 2), ("xr", 1), ("xf", 1), ("tm", 1), ("fwh", 0, 1), ("xr", 2), ("zw", 4), ("ys", 4), ("fwh", 1, 0),
-    ("fwh", 1, 1), ("yr", 3), ("yr", 5), ("xf", 2), ("xe", 0), ("xe", 1), ("mm", 0), ("xe", 2), ("back", 1),
-    ("xo", 3), ("yr", 4), ("mm", 1), ("tmh", 0), ("xr", 3), ("mm", 2), ("tmh", 1), ("mm", 3), ("xf", 3),
-    ("bkh", 0), ("xo", 4), ("ye", 0), ("ye", 1), ("ye", 7), ("ye", 2), ("ye", 6), ("ye", 3), ("ye", 5),
-    ("ye", 4), ("mm", 4), ("bkh", 1), ("xo", 5), ("xe", 3), ("xr", 4), ("mm", 5, 0), ("xr", 5), ("mm", 5, 1),
-    ("xf", 4), ("xf", 5), ("xe", 4), ("mm", 6, 0), ("xe", 5), ("mm", 6, 1),
+    ("pick", 4), ("fill",), ("zw", 1), ("zs", 2), ("ys", 1), ("ys", 7), ("fwd", 0, 2), ("fwd", 0, 3),
+    ("sp", 0), ("xo", 0), ("yw", 0), ("yr", 0), ("zw", 2), ("ys", 2), ("ys", 6), ("fwd", 1, 0), ("fwd", 1, 1),
+    ("zs", 3), ("fwd", 1, 2), ("fwd", 1, 3), ("sp", 1), ("xo", 1), ("yw", 1), ("yr", 1), ("yw", 7), ("yr", 7),
+    ("tm", 0), ("sp", 2), ("xr", 0), ("xf", 0), ("yw", 2), ("yr", 2), ("yw", 6), ("yr", 6), ("zw", 3),
+    ("zs", 4), ("ys", 3), ("ys", 5), ("fwh", 0, 0), ("xr", 1), ("xf", 1), ("back", 0), ("xo", 2), ("tm", 1),
+    ("fwh", 0, 1), ("fwh", 1, 0), ("zw", 4), ("ys", 4), ("fwh", 1, 1), ("xe", 0), ("xe", 1), ("mm", 0),
+    ("yw", 3), ("yr", 3), ("xr", 2), ("yw", 5), ("yr", 5), ("xf", 2), ("xe", 2), ("tmh", 0), ("back", 1),
+    ("xo", 3), ("yw", 4), ("yr", 4), ("mm", 1), ("tmh", 1), ("xr", 3), ("mm", 2), ("bkh", 0), ("xo", 4),
+    ("mm", 3), ("xf", 3), ("ye",), ("mm", 4), ("bkh", 1), ("xo", 5), ("xr", 4), ("xe", 3), ("mm", 5, 0),
+    ("mm", 5, 1), ("xr", 5), ("xf", 4), ("xe", 4), ("mm", 6, 0), ("xf", 5), ("xe", 5), ("mm", 6, 1),
 )
 
 
@@ -75,8 +75,8 @@
 
 
 class WeightRing:
-    def __init__(self, rows, zs, zr, ys, yr, head, y, z):
-        self.rows, self.zs, self.zr, self.ys, self.yr = rows, zs, zr, ys, yr
+    def __init__(self, rows, zs, zr, ys, yr, far, head, y, z):
+        self.rows, self.zs, self.zr, self.ys, self.yr, self.far = rows, zs, zr, ys, yr, far
         self.z = z
         self.z_next = (y * NZ + (z + 1) % NZ, head)
         self.z_prev = (y * NZ + (z + NZ - 1) % NZ, head)
@@ -92,8 +92,8 @@
     def send_z(self, t):
         up = self.block(0, NZ + 1 - t, None if t < 4 else 0)
         down = self.block(0, t - 1, None if t < 4 else 1)
-        remote(up, up, self.zs.at[0, t - 1], self.zr.at[0, t - 1], self.z_next).start()
-        remote(down, down, self.zs.at[1, t - 1], self.zr.at[1, t - 1], self.z_prev).start()
+        remote(up, up, self.zs.at[0], self.zr.at[0, t - 1], self.z_next).start()
+        remote(down, down, self.zs.at[1], self.zr.at[1, t - 1], self.z_prev).start()
 
     def wait_z(self, t):
         wait_on(self.block(0, NZ - t, None if t < 4 else 0), self.zr.at[0, t - 1])
@@ -101,32 +101,31 @@
 
     def send_y(self, dz):
         own = self.block(0, dz)
-        remote(own, self.block(3, dz), self.ys.at[0, dz], self.yr.at[0, dz], self.y_next).start()
-        remote(own, self.block(1, dz), self.ys.at[1, dz], self.yr.at[1, dz], self.y_prev).start()
+        remote(own, self.block(3, dz), self.ys.at[0], self.yr.at[0, dz], self.y_next).start()
+        remote(own, self.block(1, dz), self.ys.at[1], self.yr.at[1, dz], self.y_prev).start()
+
+    def wait_y(self, dz):
+        wait_on(self.block(3, dz), self.yr.at[0, dz])
+        wait_on(self.block(1, dz), self.yr.at[1, dz])
 
     def relay_y(self, dz):
         for way, d, to in ((0, 3, self.y_next), (1, 1, self.y_prev)):
-            wait_on(self.block(d, dz), self.yr.at[way, dz])
             remote(
                 self.block(d, dz, way),
                 self.block(2, dz, way),
-                self.ys.at[2 + way, dz],
-                self.yr.at[2 + way, dz],
+                self.ys.at[2 + way],
+                self.far,
                 to,
             ).start()
 
-    def finish_y(self, dz):
+    def finish_y(self):
+        wait_on(self.rows[2], self.far)
+
+    def drain(self):
         for way in range(2):
-            wait_on(self.block(2, dz, way), self.yr.at[2 + way, dz])
-
-    def drain(self):
-        whole, half = self.block(0, 0), self.block(0, 0, 0)
-        for t in range(1, 5):
-            for way in range(2):
-                wait_on(whole if t < 4 else half, self.zs.at[way, t - 1])
-        for dz in range(NZ):
-            for way in range(4):
-                wait_on(whole if way < 2 else half, self.ys.at[way, dz])
+            wait_on(self.rows[0].at[pl.ds(0, 35)], self.zs.at[way])
+            wait_on(self.rows[0], self.ys.at[way])
+            wait_on(self.rows[0].at[pl.ds(0, 40)], self.ys.at[2 + way])
 
 
 class AttendedRing:
@@ -144,44 +143,32 @@
         return self.groups.at[(x % NX) * 2 + core, pl.ds(k * (FRAMES // 2), FRAMES // 2)]
 
     def copy(self, ref, k, device):
-        remote(ref, ref, self.send.at[k], self.recv.at[k], device).start()
+        remote(ref, ref, self.send, self.recv.at[k], device).start()
 
     def own(self):
         mine = self.whole(self.x, self.core)
         self.copy(mine, 0, self.next)
         self.copy(mine, 1, self.prev)
-        self.copy(mine, 2, self.other)
+        self.copy(mine, 4, self.other)
 
     def relay(self):
-        came = self.whole(self.x + NX - 1, self.core)
-        wait_on(came, self.recv.at[0])
-        self.copy(self.half(self.x + NX - 1, self.core, 0), 3, self.next)
-        self.copy(came, 5, self.other)
-        came = self.whole(self.x + 1, self.core)
-        wait_on(came, self.recv.at[1])
-        self.copy(self.half(self.x + 1, self.core, 1), 4, self.prev)
-        self.copy(came, 6, self.other)
+        for way, dx, to in ((0, NX - 1, self.next), (1, 1, self.prev)):
+            came = self.whole(self.x + dx, self.core)
+            wait_on(came, self.recv.at[way])
+            self.copy(self.half(self.x + dx, self.core, way), 2 + way, to)
+            self.copy(came, 4, self.other)
 
     def relay_far(self):
-        for k in range(2):
-            came = self.half(self.x + 2, self.core, k)
-            wait_on(came, self.recv.at[3 + k])
-            self.copy(came, 7 + k, self.other)
+        for way in range(2):
+            came = self.half(self.x + 2, self.core, way)
+            wait_on(came, self.recv.at[2 + way])
+            self.copy(came, 4, self.other)
 
     def finish(self):
-        across = 1 - self.core
-        wait_on(self.whole(self.x, across), self.recv.at[2])
-        wait_on(self.whole(self.x + NX - 1, across), self.recv.at[5])
-        wait_on(self.whole(self.x + 1, across), self.recv.at[6])
-        wait_on(self.half(self.x + 2, across, 0), self.recv.at[7])
-        wait_on(self.half(self.x + 2, across, 1), self.recv.at[8])
+        wait_on(self.groups.at[pl.ds(0, 4)], self.recv.at[4])
 
     def drain(self):
-        whole, half = self.whole(self.x, self.core), self.half(self.x, self.core, 0)
-        for k in (0, 1, 2, 5, 6):
-            wait_on(whole, self.send.at[k])
-        for k in (3, 4, 7, 8):
-            wait_on(half, self.send.at[k])
+        wait_on(self.groups.at[pl.ds(0, 7)], self.send)
 
 
 def softmax_rows(scores):
@@ -226,6 +213,7 @@
     wz_recv,
     wy_send,
     wy_recv,
+    far_recv,
     x_send,
     x_recv,
 ):
@@ -234,21 +222,13 @@
     weight = (weight0, weight1, weight2, weight3)
     x, core = head // 2, head % 2
 
-    loads = [
-        pltpu.make_async_copy(
-            w_hbm.at[pl.ds(n * 16, 16), :], weight0.at[z * 10 + n], load_sem.at[3, n]
-        )
-        for n in range(10)
-    ]
-    loads += [
-        pltpu.make_async_copy(
-            source.at[:, pl.ds(h * HDIM, HDIM)], heads_in.at[n, h], load_sem.at[n, h]
-        )
-        for n, source in enumerate((q_hbm, k_hbm, v_hbm))
-        for h in range(HEAD_DEV)
-    ]
-    for load in loads:
-        load.start()
+    load_weight = pltpu.make_async_copy(w_hbm, weight0.at[pl.ds(z * 10, 10)], load_sem.at[0])
+    load_weight.start()
+    for n, source in enumerate((q_hbm, k_hbm, v_hbm)):
+        for h in range(HEAD_DEV):
+            pltpu.make_async_copy(
+                source.at[:, pl.ds(h * HDIM, HDIM)], heads_in.at[n, h], load_sem.at[1]
+            ).start()
 
     barrier = pltpu.get_barrier_semaphore()
 
@@ -275,22 +255,21 @@
             )
         table[line * 8 + HEAD_DEV] = temporal_count - 2
 
-    fill(head, 0)
-    for g in range(GROUPS):
-        fill(g, 1 + g)
+    def fill_all():
+        for g in range(GROUPS):
+            fill(g, 1 + g)
 
     def pick(slot):
         if slot == SLOT_EITHER:
-            for load in loads[10:]:
-                load.wait()
+            wait_on(heads_in, load_sem.at[1])
         for n in range(3):
             slots[slot, n] = heads_in[n, table[slot]].reshape(TILED)
 
-    for load in loads[:10]:
-        load.wait()
+    fill(head, 0)
+    load_weight.wait()
     pl.semaphore_wait(barrier, FRAMES - 1 + 3)
 
-    ring = WeightRing(weight, wz_send, wz_recv, wy_send, wy_recv, head, y, z)
+    ring = WeightRing(weight, wz_send, wz_recv, wy_send, wy_recv, far_recv.at[0], head, y, z)
     gather = [
         AttendedRing(ref, x_send.at[n], x_recv.at[n], frame, x, core)
         for n, ref in enumerate(
@@ -432,9 +411,11 @@
 
     acts = {
         "pick": pick,
+        "fill": fill_all,
         "zs": ring.send_z,
         "zw": ring.wait_z,
         "ys": ring.send_y,
+        "yw": ring.wait_y,
         "yr": ring.relay_y,
         "ye": ring.finish_y,
         "fwd": forward,
@@ -490,24 +471,25 @@
             pltpu.VMEM((GROUPS * HDIM, COLS), BF16),
             pltpu.VMEM((FRAMES, 2, HALF, COLS), F32),
             pltpu.VMEM((FRAMES, 2, HALF, COLS), BF16),
-            dma((4, 10)),
+            dma((2,)),
             dma((2,)),
             dma((4,)),
             dma((4,)),
             dma((4,)),
             dma((4,)),
+            dma((2,)),
             dma((2, 4)),
-            dma((2, 4)),
-            dma((4, NZ)),
-            dma((4, NZ)),
-            dma((HEAD_DEV + 1, 9)),
-            dma((HEAD_DEV + 1, 9)),
+            dma((4,)),
+            dma((2, NZ)),
+            dma((1,)),
+            dma((HEAD_DEV + 1,)),
+            dma((HEAD_DEV + 1, 5)),
         ],
         compiler_params=pltpu.CompilerParams(
             collective_id=0, has_side_effects=True, vmem_limit_bytes=56 << 20
         ),
         name="block_kernel",
-    )(head_labels, queries, key_states, value_states, out_weight).reshape(POS, COLS)
+    )(head_labels, queries, key_states, value_states, out_weight.reshape(10, 16, COLS)).reshape(POS, COLS)
 
 
 def solution(mesh):

time: 119 us -> 116 us (0.975)
  Pallas kernels: 118 us -> 115 us
    pallas_call x1, Pallas kernels: 118 us -> 115 us  [per_device(): pl.pallas_call(block_kernel, out_shape=pltpu.VMEM((FRAMES, 2, HALF, COLS)...]
where the time goes in v3:
time: 116 us
  Pallas kernels  115 us (99%)
    pallas_call x1, Pallas kernels, per_device(): pl.pallas_call(block_kernel, out_shape=pltpu.VMEM((FRAMES, 2, HALF, COLS)...  115 us

profile of v3, /device:TPU:1, one launch (start us, length us, event | category | flops | bytes accessed | tf_op | source)
XLA Modules:
  0.0 115.8 jit_solution(7385708238519472720)
XLA Ops:
  0.0 114.7 %block_kernel.1 = bf16[32,2,16,640]{3,2,1,0:T(8,128)(2,1)S(1)} custom-call(s32[40]{0:T(128)} %labels.1, bf16[1024,640]{1,0:T(8,128)(2,1)} %q_hbm.1, bf16[1024,640]{1,0:T(8,128)(2,1)} %k_hbm.1, bf16[1024,640]{1,0:T(8,128)(2,1)} %v_hbm.1, bf16[10,16,640]{2,1,0:T(8,128)(2,1)} %bitcast.3), custom_call_target="tpu_custom_call" | custom-call | tf_op jit(solution)/shard_map/block_kernel/pallas_call | solution.py:453
  114.8 1.1 copy.7

commit v4 on v3

--- a/solution.py
+++ b/solution.py
@@ -22,6 +22,7 @@
 COLS = 640
 EXP_SCALE = HDIM**-0.5 * math.log2(math.e)
 NEG = -1e30
+SPLIT_FROM = 4
 HALF = PB // 2
 TILED = (FRAMES, 2, HALF, HDIM)
 
@@ -36,7 +37,7 @@
     ("tm", 0), ("sp", 2), ("xr", 0), ("xf", 0), ("yw", 2), ("yr", 2), ("yw", 6), ("yr", 6), ("zw", 3),
     ("zs", 4), ("ys", 3), ("ys", 5), ("fwh", 0, 0), ("xr", 1), ("xf", 1), ("back", 0), ("xo", 2), ("tm", 1),
     ("fwh", 0, 1), ("fwh", 1, 0), ("zw", 4), ("ys", 4), ("fwh", 1, 1), ("xe", 0), ("xe", 1), ("mm", 0),
-    ("yw", 3), ("yr", 3), ("xr", 2), ("yw", 5), ("yr", 5), ("xf", 2), ("xe", 2), ("tmh", 0), ("back", 1),
+    ("yw", 3), ("yr", 3), ("xr", 2), ("xf", 2), ("yw", 5), ("yr", 5), ("xe", 2), ("tmh", 0), ("back", 1),
     ("xo", 3), ("yw", 4), ("yr", 4), ("mm", 1), ("tmh", 1), ("xr", 3), ("mm", 2), ("bkh", 0), ("xo", 4),
     ("mm", 3), ("xf", 3), ("ye",), ("mm", 4), ("bkh", 1), ("xo", 5), ("xr", 4), ("xe", 3), ("mm", 5, 0),
     ("mm", 5, 1), ("xr", 5), ("xf", 4), ("xe", 4), ("mm", 6, 0), ("xf", 5), ("xe", 5), ("mm", 6, 1),
@@ -129,8 +130,8 @@
 
 
 class AttendedRing:
-    def __init__(self, groups, send, recv, frame, x, core):
-        self.groups, self.send, self.recv = groups, send, recv
+    def __init__(self, groups, send, recv, split, frame, x, core):
+        self.groups, self.send, self.recv, self.split = groups, send, recv, split
         self.x, self.core = x, core
         self.next = (frame, ((x + 1) % NX) * 2 + core)
         self.prev = (frame, ((x + NX - 1) % NX) * 2 + core)
@@ -147,16 +148,27 @@
 
     def own(self):
         mine = self.whole(self.x, self.core)
-        self.copy(mine, 0, self.next)
-        self.copy(mine, 1, self.prev)
+        for first in range(2) if self.split else (None,):
+            for way, to in ((0, self.next), (1, self.prev)):
+                if first is None:
+                    self.copy(mine, way, to)
+                else:
+                    part = (way + first) % 2
+                    self.copy(self.half(self.x, self.core, part), 5 * first + way, to)
         self.copy(mine, 4, self.other)
 
     def relay(self):
-        for way, dx, to in ((0, NX - 1, self.next), (1, 1, self.prev)):
-            came = self.whole(self.x + dx, self.core)
-            wait_on(came, self.recv.at[way])
-            self.copy(self.half(self.x + dx, self.core, way), 2 + way, to)
-            self.copy(came, 4, self.other)
+        ways = ((0, NX - 1, self.next), (1, 1, self.prev))
+        for way, dx, to in ways:
+            came, part = self.whole(self.x + dx, self.core), self.half(self.x + dx, self.core, way)
+            wait_on(part if self.split else came, self.recv.at[way])
+            self.copy(part, 2 + way, to)
+            if not self.split:
+                self.copy(came, 4, self.other)
+        if self.split:
+            for way, dx, to in ways:
+                wait_on(self.half(self.x + dx, self.core, 1 - way), self.recv.at[5 + way])
+                self.copy(self.whole(self.x + dx, self.core), 4, self.other)
 
     def relay_far(self):
         for way in range(2):
@@ -189,6 +201,7 @@
     w_hbm,
     out,
     table,
+    apart,
     heads_in,
     slots,
     got,
@@ -258,6 +271,9 @@
     def fill_all():
         for g in range(GROUPS):
             fill(g, 1 + g)
+        row_at = lax.broadcasted_iota(jnp.int32, apart.shape, 0) % HALF
+        col_at = lax.broadcasted_iota(jnp.int32, apart.shape, 1) % HALF
+        apart[...] = jnp.where(row_at == col_at, 0.0, NEG)
 
     def pick(slot):
         if slot == SLOT_EITHER:
@@ -271,7 +287,7 @@
 
     ring = WeightRing(weight, wz_send, wz_recv, wy_send, wy_recv, far_recv.at[0], head, y, z)
     gather = [
-        AttendedRing(ref, x_send.at[n], x_recv.at[n], frame, x, core)
+        AttendedRing(ref, x_send.at[n], x_recv.at[n], n >= SPLIT_FROM, frame, x, core)
         for n, ref in enumerate(
             [gathered.at[slot] for slot in range(4)] + [gathered.at[4, :, :, h] for h in range(2)]
         )
@@ -339,10 +355,8 @@
 
     def temporal(s, h):
         rows = FRAMES * HALF
-        row_at = lax.broadcasted_iota(jnp.int32, (rows, rows), 0) % HALF
-        col_at = lax.broadcasted_iota(jnp.int32, (rows, rows), 1) % HALF
         query, key, value = (got[s, n, :, h].reshape(rows, HDIM) for n in range(3))
-        expo, row_sum = softmax_rows(jnp.where(row_at == col_at, dot_t(query, key), NEG))
+        expo, row_sum = softmax_rows(dot_t(query, key) + apart[...])
         mix = jnp.dot(expo, value, preferred_element_type=F32)
         mixed[s, :, h] = (mix / row_sum).astype(BF16).reshape(FRAMES, HALF, HDIM)
 
@@ -457,6 +471,7 @@
         out_specs=any_spec,
         scratch_shapes=[
             pltpu.SMEM(((1 + GROUPS) * 8,), jnp.int32),
+            pltpu.VMEM((FRAMES * HALF, FRAMES * HALF), F32),
             pltpu.VMEM((3, HEAD_DEV, POS, HDIM), BF16),
             pltpu.VMEM((HEAD_DEV, 3) + TILED, BF16),
             pltpu.VMEM((3, 3) + TILED, BF16),
@@ -483,7 +498,7 @@
             dma((2, NZ)),
             dma((1,)),
             dma((HEAD_DEV + 1,)),
-            dma((HEAD_DEV + 1, 5)),
+            dma((HEAD_DEV + 1, 7)),
         ],
         compiler_params=pltpu.CompilerParams(
             collective_id=0, has_side_effects=True, vmem_limit_bytes=56 << 20

time: 116 us -> 115 us (level)
  no operation moved by 1% of the time
where the time goes in v4:
time: 115 us
  Pallas kernels  114 us (99%)
    pallas_call x1, Pallas kernels, per_device(): pl.pallas_call(block_kernel, out_shape=pltpu.VMEM((FRAMES, 2, HALF, COLS)...  114 us

profile of v4, /device:TPU:1, one launch (start us, length us, event | category | flops | bytes accessed | tf_op | source)
XLA Modules:
  0.0 115.3 jit_solution(5349713275510418292)
XLA Ops:
  0.0 114.2 %block_kernel.1 = bf16[32,2,16,640]{3,2,1,0:T(8,128)(2,1)S(1)} custom-call(s32[40]{0:T(128)} %labels.1, bf16[1024,640]{1,0:T(8,128)(2,1)} %q_hbm.1, bf16[1024,640]{1,0:T(8,128)(2,1)} %k_hbm.1, bf16[1024,640]{1,0:T(8,128)(2,1)} %v_hbm.1, bf16[10,16,640]{2,1,0:T(8,128)(2,1)} %bitcast.3), custom_call_target="tpu_custom_call" | custom-call | tf_op jit(solution)/shard_map/block_kernel/pallas_call | solution.py:467
  114.3 1.1 copy.7

commit v5 on v4

--- a/solution.py
+++ b/solution.py
@@ -35,7 +35,7 @@
     ("sp", 0), ("xo", 0), ("yw", 0), ("yr", 0), ("zw", 2), ("ys", 2), ("ys", 6), ("fwd", 1, 0), ("fwd", 1, 1),
     ("zs", 3), ("fwd", 1, 2), ("fwd", 1, 3), ("sp", 1), ("xo", 1), ("yw", 1), ("yr", 1), ("yw", 7), ("yr", 7),
     ("tm", 0), ("sp", 2), ("xr", 0), ("xf", 0), ("yw", 2), ("yr", 2), ("yw", 6), ("yr", 6), ("zw", 3),
-    ("zs", 4), ("ys", 3), ("ys", 5), ("fwh", 0, 0), ("xr", 1), ("xf", 1), ("back", 0), ("xo", 2), ("tm", 1),
+    ("ys", 3), ("ys", 5), ("zs", 4), ("fwh", 0, 0), ("xr", 1), ("xf", 1), ("back", 0), ("xo", 2), ("tm", 1),
     ("fwh", 0, 1), ("fwh", 1, 0), ("zw", 4), ("ys", 4), ("fwh", 1, 1), ("xe", 0), ("xe", 1), ("mm", 0),
     ("yw", 3), ("yr", 3), ("xr", 2), ("xf", 2), ("yw", 5), ("yr", 5), ("xe", 2), ("tmh", 0), ("back", 1),
     ("xo", 3), ("yw", 4), ("yr", 4), ("mm", 1), ("tmh", 1), ("xr", 3), ("mm", 2), ("bkh", 0), ("xo", 4),

time: 115 us -> 115 us (level)
  no operation moved by 1% of the time
where the time goes in v5:
time: 115 us
  Pallas kernels  114 us (99%)
    pallas_call x1, Pallas kernels, per_device(): pl.pallas_call(block_kernel, out_shape=pltpu.VMEM((FRAMES, 2, HALF, COLS)...  114 us

profile of v5, /device:TPU:1, one launch (start us, length us, event | category | flops | bytes accessed | tf_op | source)
XLA Modules:
  0.0 115.3 jit_solution(7880847248968476809)
XLA Ops:
  0.0 114.2 %block_kernel.1 = bf16[32,2,16,640]{3,2,1,0:T(8,128)(2,1)S(1)} custom-call(s32[40]{0:T(128)} %labels.1, bf16[1024,640]{1,0:T(8,128)(2,1)} %q_hbm.1, bf16[1024,640]{1,0:T(8,128)(2,1)} %k_hbm.1, bf16[1024,640]{1,0:T(8,128)(2,1)} %v_hbm.1, bf16[10,16,640]{2,1,0:T(8,128)(2,1)} %bitcast.3), custom_call_target="tpu_custom_call" | custom-call | tf_op jit(solution)/shard_map/block_kernel/pallas_call | solution.py:467
  114.3 1.1 copy.7
